TPU v7x, 512 devices: a whole 4x4x16 slice. The times are simulated.
512 devices in a mesh: dp: 512 (over x, z, y, core).
Axes of the slice: x: 4, y: 4, z: 16, core: 2. Of those that a mesh axis runs over, the one named last changes fastest.
Arguments:
- image_feats: bfloat16 [65536, 640], P('dp'), may hold values from -6 to 6
- proj_head: bfloat16 [640, 1152], replicated, may hold values from -0.0068359375 to 0.0068359375
- rest_part: bfloat16 [65536, 1152], P('dp'), may hold values from -0.19921875 to 0.19921875
- text_embed: bfloat16 [65536, 1152], P('dp'), may hold values from -0.19921875 to 0.19921875
- logit_scale: float32 [1], replicated, may hold values from 5 to 15
- logit_bias: float32 [1], replicated, may hold values from -4 to -2
Outputs:
- grad_text: bfloat16 [65536, 1152], P('dp')
- grad_proj: bfloat16 [640, 1152], replicated
All inputs are finite; a program needn't handle non-finite values.
Results may differ from a plain program's by a relative error of at most 0.0065.
Values may be sent and summed in bfloat16 or wider, within the bound.
A program may use at most 64 MiB of HBM per device.

v0:
```python
import jax
import jax.numpy as jnp
from jax import lax
from jax.sharding import PartitionSpec as P

STEPS = 8


def from_behind(block, axis, distance):
    devices = range(lax.axis_size(axis))
    route = [((i - distance) % len(devices), i) for i in devices]
    return lax.ppermute(block, axis, route)


def unit_rows(raw):
    values = raw.astype(jnp.float32)
    squares = jnp.sum(values * values, axis=-1, keepdims=True) + 1e-06
    return (values, squares, (values / jnp.sqrt(squares)).astype(jnp.bfloat16))


def back_norm(values, squares, grads):
    inner = jnp.sum(values * grads, axis=-1, keepdims=True)
    return (grads - values * inner / squares) / jnp.sqrt(squares)


def coefficients(left, right, scale, bias, first):
    logits = (
        scale
        * lax.dot_general(left, right, (((1,), (1,)), ((), ())), preferred_element_type=jnp.float32)
        + bias
    )
    rows = left.shape[0]
    if first:
        label = 2.0 * jnp.eye(rows, dtype=jnp.float32) - 1.0
    else:
        label = -jnp.ones((rows, rows), jnp.float32)
    return (-label * scale * jax.nn.sigmoid(-label * logits)).astype(jnp.bfloat16)


def transposed(coef, block):
    return lax.dot_general(
        coef, block, (((0,), (0,)), ((), ())), preferred_element_type=jnp.float32
    )


def on_device(image_feats, proj_head, rest_part, text_embed, logit_scale, logit_bias):
    scale = logit_scale[0]
    bias = logit_bias[0]
    y_full = jnp.dot(image_feats, proj_head, preferred_element_type=jnp.float32) + rest_part.astype(
        jnp.float32
    )
    y_vals, y_sq, image_unit = unit_rows(y_full)
    t_vals, t_sq, text_unit = unit_rows(text_embed)
    grad_image = jnp.zeros(y_vals.shape, jnp.float32)
    text_now = text_unit
    pending = jnp.zeros(t_vals.shape, jnp.float32)
    for step in range(STEPS):
        if step > 0:
            text_now = from_behind(text_now, "dp", 1)
            pending = from_behind(pending, "dp", 1)
        coef = coefficients(image_unit, text_now, scale, bias, step == 0)
        grad_image = grad_image + jnp.dot(coef, text_now, preferred_element_type=jnp.float32)
        pending = pending + transposed(coef, image_unit)
    grad_texts = from_behind(pending, "dp", -(STEPS - 1))
    grad_y = back_norm(y_vals, y_sq, grad_image).astype(jnp.bfloat16)
    head_local = transposed(image_feats, grad_y)
    head_total = lax.psum(head_local, "dp")
    grad_proj = (head_total / lax.axis_size("dp")).astype(jnp.bfloat16)
    grad_text = back_norm(t_vals, t_sq, grad_texts).astype(jnp.bfloat16)
    return (grad_text, grad_proj)


def solution(mesh):
    placed = (P("dp", None), P(), P("dp", None), P("dp", None), P(), P())
    return jax.shard_map(
        on_device, mesh=mesh, in_specs=placed, out_specs=(P("dp", None), P()), check_vma=False
    )
```

profile of v0, /device:TPU:1, one launch (start us, length us, event | category | flops | bytes accessed | tf_op | source)
XLA Modules:
  0.0 608.7 jit_solution(7836083413587608659)
XLA Ops:
  7.2 1.2 fusion.57
  9.5 4.6 collective-permute-start.1
  14.1 1.6 multiply_reduce_fusion.1
  17.7 1.9 collective-permute-start
  19.9 3.6 collective-permute-start.3
  24.0 2.5 collective-permute-done
  26.7 4.4 collective-permute-start.2
  31.1 2.8 collective-permute-done.3
  33.9 1.9 collective-permute-start.5
  36.6 10.8 %collective-permute-done.5 = bf16[128,1152]{1,0:T(8,128)(2,1)S(1)} collective-permute-done((bf16[128,1152]{1,0:T(8,128)(2,1)S(1)}, bf16[128,1152]{1,0:T(8,128)(2,1)S(1)}, u32[]{:S(2)}, u32[]{:S(2)}) %collective-permute-start.5) | collective-permute-done | bytes 294944 | tf_op jit(solution)/shard_map/ppermute | solution.py:12
  47.4 1.9 collective-permute-start.7
  50.1 1.9 collective-permute-start.4
  52.0 10.6 %collective-permute-done.7 = bf16[128,1152]{1,0:T(8,128)(2,1)S(1)} collective-permute-done((bf16[128,1152]{1,0:T(8,128)(2,1)S(1)}, bf16[128,1152]{1,0:T(8,128)(2,1)S(1)}, u32[]{:S(2)}, u32[]{:S(2)}) %collective-permute-start.7) | collective-permute-done | bytes 294944 | tf_op jit(solution)/shard_map/ppermute | solution.py:12
  62.6 1.9 collective-permute-start.9
  65.3 10.8 %collective-permute-done.9 = bf16[128,1152]{1,0:T(8,128)(2,1)S(1)} collective-permute-done((bf16[128,1152]{1,0:T(8,128)(2,1)S(1)}, bf16[128,1152]{1,0:T(8,128)(2,1)S(1)}, u32[]{:S(2)}, u32[]{:S(2)}) %collective-permute-start.9) | collective-permute-done | bytes 294944 | tf_op jit(solution)/shard_map/ppermute | solution.py:12
  76.1 1.9 collective-permute-start.11
  78.6 1.9 collective-permute-start.6
  80.5 9.0 %collective-permute-done.11 = bf16[128,1152]{1,0:T(8,128)(2,1)S(1)} collective-permute-done((bf16[128,1152]{1,0:T(8,128)(2,1)S(1)}, bf16[128,1152]{1,0:T(8,128)(2,1)S(1)}, u32[]{:S(2)}, u32[]{:S(2)}) %collective-permute-start.11) | collective-permute-done | bytes 294944 | tf_op jit(solution)/shard_map/ppermute | solution.py:12
  89.5 1.9 collective-permute-start.13
  91.9 11.0 %collective-permute-done.13 = bf16[128,1152]{1,0:T(8,128)(2,1)S(1)} collective-permute-done((bf16[128,1152]{1,0:T(8,128)(2,1)S(1)}, bf16[128,1152]{1,0:T(8,128)(2,1)S(1)}, u32[]{:S(2)}, u32[]{:S(2)}) %collective-permute-start.13) | collective-permute-done | bytes 294944 | tf_op jit(solution)/shard_map/ppermute | solution.py:12
  103.7 1.9 collective-permute-start.8
  105.6 2.3 convolution_bitcast_fusion
  108.2 9.4 %collective-permute-done.8 = f32[128,1152]{1,0:T(8,128)S(1)} collective-permute-done((f32[128,1152]{1,0:T(8,128)S(1)}, f32[128,1152]{1,0:T(8,128)S(1)}, u32[]{:S(2)}, u32[]{:S(2)}) %collective-permute-start.8) | collective-permute-done | bytes 589856 | tf_op jit(solution)/shard_map/ppermute | solution.py:12
  117.6 1.9 collective-permute-start.10
  119.8 14.5 %collective-permute-done.10 = f32[128,1152]{1,0:T(8,128)S(1)} collective-permute-done((f32[128,1152]{1,0:T(8,128)S(1)}, f32[128,1152]{1,0:T(8,128)S(1)}, u32[]{:S(2)}, u32[]{:S(2)}) %collective-permute-start.10) | collective-permute-done | bytes 589856 | tf_op jit(solution)/shard_map/ppermute | solution.py:12
  134.4 1.9 collective-permute-start.12
  136.6 15.2 %collective-permute-done.12 = f32[128,1152]{1,0:T(8,128)S(1)} collective-permute-done((f32[128,1152]{1,0:T(8,128)S(1)}, f32[128,1152]{1,0:T(8,128)S(1)}, u32[]{:S(2)}, u32[]{:S(2)}) %collective-permute-start.12) | collective-permute-done | bytes 589856 | tf_op jit(solution)/shard_map/ppermute | solution.py:12
  152.7 1.9 collective-permute-start.14
  154.7 439.8 %all-reduce.2.cloned.1.call-done = f32[640,1152]{0,1:T(8,128)} async-done(((f32[640,1152]{0,1:T(8,128)}), f32[640,1152]{0,1:T(8,128)}) %all-reduce.2.cloned.1.call-update) | async-done | bytes 2949136 | tf_op jit(solution)/shard_map/psum | solution.py:67
  594.5 2.1 multiply_convert_fusion
  596.5 2.1 copy.8
  599.8 2.0 fusion.63
  (48 shorter events, 9.8 us)
Async XLA Ops:
  7.2 7.0 %copy-start = (bf16[640,1152]{1,0:T(8,128)(2,1)S(1)}, bf16[640,1152]{1,0:T(8,128)(2,1)}, u32[]{:S(2)}) copy-start(bf16[640,1152]{1,0:T(8,128)(2,1)} %param.7) | copy-start | bytes 4423684
  7.2 587.3 %all-reduce.2.cloned.1.call-start = ((), (), s32[]{:S(2)}) async-start(), calls=%async_computation | async-start | bytes 5898240 | tf_op jit(solution)/shard_map/psum | solution.py:67
  9.5 10.3 %collective-permute-start.1 = (bf16[128,1152]{1,0:T(8,128)(2,1)S(1)}, bf16[128,1152]{1,0:T(8,128)(2,1)S(1)}, u32[]{:S(2)}, u32[]{:S(2)}) collective-permute-start(bf16[128,1152]{1,0:T(8,128)(2,1)S(1)} %fusion.58), channel_id=1, source_target_pairs={{511,0},{0,1},{1,2},{2,3},{3,4},{4,5},{5,6},{6,7},{7,8},{8,9},{9,1... | collective-permute-start | bytes 884744 | tf_op jit(solution)/shard_map/ppermute | solution.py:12
  17.7 8.7 %collective-permute-start = (f32[128,1152]{1,0:T(8,128)S(1)}, f32[128,1152]{1,0:T(8,128)S(1)}, u32[]{:S(2)}, u32[]{:S(2)}) collective-permute-start(f32[128,1152]{1,0:T(8,128)S(1)} %fusion.69), channel_id=1, source_target_pairs={{511,0},{0,1},{1,2},{2,3},{3,4},{4,5},{5,6},{6,7},{7,8},{8,9},{9,1... | collective-permute-start | bytes 1769480 | tf_op jit(solution)/shard_map/ppermute | solution.py:12
  19.9 14.0 %collective-permute-start.3 = (bf16[128,1152]{1,0:T(8,128)(2,1)S(1)}, bf16[128,1152]{1,0:T(8,128)(2,1)S(1)}, u32[]{:S(2)}, u32[]{:S(2)}) collective-permute-start(bf16[128,1152]{1,0:T(8,128)(2,1)S(1)} %collective-permute-done.1), channel_id=1, source_target_pairs={{511,0},{0,1},{1,2},{2,3},{3,4},{4,5},{5,6},{6,7},{7,8},{8,9},{9,1... | collective-permute-start | bytes 884744 | tf_op jit(solution)/shard_map/ppermute | solution.py:12
  26.7 23.3 %collective-permute-start.2 = (f32[128,1152]{1,0:T(8,128)S(1)}, f32[128,1152]{1,0:T(8,128)S(1)}, u32[]{:S(2)}, u32[]{:S(2)}) collective-permute-start(f32[128,1152]{1,0:T(8,128)S(1)} %convolution_add_fusion.7), channel_id=1, source_target_pairs={{511,0},{0,1},{1,2},{2,3},{3,4},{4,5},{5,6},{6,7},{7,8},{8,9},{9,1... | collective-permute-start | bytes 1769480 | tf_op jit(solution)/shard_map/ppermute | solution.py:12
  33.9 13.5 %collective-permute-start.5 = (bf16[128,1152]{1,0:T(8,128)(2,1)S(1)}, bf16[128,1152]{1,0:T(8,128)(2,1)S(1)}, u32[]{:S(2)}, u32[]{:S(2)}) collective-permute-start(bf16[128,1152]{1,0:T(8,128)(2,1)S(1)} %collective-permute-done.3), channel_id=1, source_target_pairs={{511,0},{0,1},{1,2},{2,3},{3,4},{4,5},{5,6},{6,7},{7,8},{8,9},{9,1... | collective-permute-start | bytes 884744 | tf_op jit(solution)/shard_map/ppermute | solution.py:12
  47.4 15.2 %collective-permute-start.7 = (bf16[128,1152]{1,0:T(8,128)(2,1)S(1)}, bf16[128,1152]{1,0:T(8,128)(2,1)S(1)}, u32[]{:S(2)}, u32[]{:S(2)}) collective-permute-start(bf16[128,1152]{1,0:T(8,128)(2,1)S(1)} %collective-permute-done.5), channel_id=1, source_target_pairs={{511,0},{0,1},{1,2},{2,3},{3,4},{4,5},{5,6},{6,7},{7,8},{8,9},{9,1... | collective-permute-start | bytes 884744 | tf_op jit(solution)/shard_map/ppermute | solution.py:12
  50.1 28.4 %collective-permute-start.4 = (f32[128,1152]{1,0:T(8,128)S(1)}, f32[128,1152]{1,0:T(8,128)S(1)}, u32[]{:S(2)}, u32[]{:S(2)}) collective-permute-start(f32[128,1152]{1,0:T(8,128)S(1)} %add.139), channel_id=1, source_target_pairs={{511,0},{0,1},{1,2},{2,3},{3,4},{4,5},{5,6},{6,7},{7,8},{8,9},{9,1... | collective-permute-start | bytes 1769480 | tf_op jit(solution)/shard_map/ppermute | solution.py:12
  62.6 13.5 %collective-permute-start.9 = (bf16[128,1152]{1,0:T(8,128)(2,1)S(1)}, bf16[128,1152]{1,0:T(8,128)(2,1)S(1)}, u32[]{:S(2)}, u32[]{:S(2)}) collective-permute-start(bf16[128,1152]{1,0:T(8,128)(2,1)S(1)} %collective-permute-done.7), channel_id=1, source_target_pairs={{511,0},{0,1},{1,2},{2,3},{3,4},{4,5},{5,6},{6,7},{7,8},{8,9},{9,1... | collective-permute-start | bytes 884744 | tf_op jit(solution)/shard_map/ppermute | solution.py:12
  76.1 13.5 %collective-permute-start.11 = (bf16[128,1152]{1,0:T(8,128)(2,1)S(1)}, bf16[128,1152]{1,0:T(8,128)(2,1)S(1)}, u32[]{:S(2)}, u32[]{:S(2)}) collective-permute-start(bf16[128,1152]{1,0:T(8,128)(2,1)S(1)} %collective-permute-done.9), channel_id=1, source_target_pairs={{511,0},{0,1},{1,2},{2,3},{3,4},{4,5},{5,6},{6,7},{7,8},{8,9},{9,1... | collective-permute-start | bytes 884744 | tf_op jit(solution)/shard_map/ppermute | solution.py:12
  78.6 25.0 %collective-permute-start.6 = (f32[128,1152]{1,0:T(8,128)S(1)}, f32[128,1152]{1,0:T(8,128)S(1)}, u32[]{:S(2)}, u32[]{:S(2)}) collective-permute-start(f32[128,1152]{1,0:T(8,128)S(1)} %add.142), channel_id=1, source_target_pairs={{511,0},{0,1},{1,2},{2,3},{3,4},{4,5},{5,6},{6,7},{7,8},{8,9},{9,1... | collective-permute-start | bytes 1769480 | tf_op jit(solution)/shard_map/ppermute | solution.py:12
  89.5 13.5 %collective-permute-start.13 = (bf16[128,1152]{1,0:T(8,128)(2,1)S(1)}, bf16[128,1152]{1,0:T(8,128)(2,1)S(1)}, u32[]{:S(2)}, u32[]{:S(2)}) collective-permute-start(bf16[128,1152]{1,0:T(8,128)(2,1)S(1)} %collective-permute-done.11), channel_id=1, source_target_pairs={{511,0},{0,1},{1,2},{2,3},{3,4},{4,5},{5,6},{6,7},{7,8},{8,9},{9,1... | collective-permute-start | bytes 884744 | tf_op jit(solution)/shard_map/ppermute | solution.py:12
  103.3 2.4 copy-start.2
  103.7 13.9 %collective-permute-start.8 = (f32[128,1152]{1,0:T(8,128)S(1)}, f32[128,1152]{1,0:T(8,128)S(1)}, u32[]{:S(2)}, u32[]{:S(2)}) collective-permute-start(f32[128,1152]{1,0:T(8,128)S(1)} %add.145), channel_id=1, source_target_pairs={{511,0},{0,1},{1,2},{2,3},{3,4},{4,5},{5,6},{6,7},{7,8},{8,9},{9,1... | collective-permute-start | bytes 1769480 | tf_op jit(solution)/shard_map/ppermute | solution.py:12
  117.6 16.7 %collective-permute-start.10 = (f32[128,1152]{1,0:T(8,128)S(1)}, f32[128,1152]{1,0:T(8,128)S(1)}, u32[]{:S(2)}, u32[]{:S(2)}) collective-permute-start(f32[128,1152]{1,0:T(8,128)S(1)} %add.148), channel_id=1, source_target_pairs={{511,0},{0,1},{1,2},{2,3},{3,4},{4,5},{5,6},{6,7},{7,8},{8,9},{9,1... | collective-permute-start | bytes 1769480 | tf_op jit(solution)/shard_map/ppermute | solution.py:12
  134.4 17.4 %collective-permute-start.12 = (f32[128,1152]{1,0:T(8,128)S(1)}, f32[128,1152]{1,0:T(8,128)S(1)}, u32[]{:S(2)}, u32[]{:S(2)}) collective-permute-start(f32[128,1152]{1,0:T(8,128)S(1)} %add.151), channel_id=1, source_target_pairs={{511,0},{0,1},{1,2},{2,3},{3,4},{4,5},{5,6},{6,7},{7,8},{8,9},{9,1... | collective-permute-start | bytes 1769480 | tf_op jit(solution)/shard_map/ppermute | solution.py:12
  152.7 445.9 %collective-permute-start.14 = (f32[128,1152]{1,0:T(8,128)}, f32[128,1152]{1,0:T(8,128)}, u32[]{:S(2)}, u32[]{:S(2)}) collective-permute-start(f32[128,1152]{1,0:T(8,128)} %add.154), channel_id=1, source_target_pairs={{7,0},{8,1},{9,2},{10,3},{11,4},{12,5},{13,6},{14,7},{15,8},{16,9}... | collective-permute-start | bytes 1769480 | tf_op jit(solution)/shard_map/ppermute | solution.py:12
  596.5 2.1 copy-start.1
Sparse Core Ops, SparseCore 0:
  108.1 486.3 all-reduce.1
where the time goes:
time: 610 us; the launch traced here: 609 us
  waiting for transfers between devices  536 us (88%)
  starting transfers between devices  35.6 us (6%)
  between operations  15.8 us (3%)
  matrix products  9.94 us (2%)
  other arithmetic  8.86 us (1%)
    psum x1, waiting for transfers between devices, on_device(): head_total = lax.psum(head_local, 'dp')  440 us
    ppermute x15, waiting for transfers between devices, from_behind(): return lax.ppermute(block, axis, route)  96.6 us
    ppermute x15, starting transfers between devices, from_behind(): return lax.ppermute(block, axis, route)  35.6 us
  transfers between devices with their start and end apart: 16, of which 11 were waited for; matrix products, arithmetic and copies ran while one was open for 3% of the time, Pallas kernels for 0%

commit v1 on v0

v1 whole, which is shorter than its diff:
```python
import jax
import jax.numpy as jnp
from jax import lax
from jax.experimental import pallas as pl
from jax.experimental.pallas import tpu as pltpu
from jax.sharding import PartitionSpec as P

D = 1152
F = 640
B = 128
N = 512
MESH = pl.DeviceIdType.MESH
ROWS = 144
TILES = 45
OWN = 12
PAD = 48


def unit_rows(values):
    squares = jnp.sum(values * values, axis=-1, keepdims=True) + 1e-06
    return squares, (values / jnp.sqrt(squares)).astype(jnp.bfloat16)


def back_norm(values, squares, grads):
    inner = jnp.sum(values * grads, axis=-1, keepdims=True)
    return (grads - values * (inner / squares)) / jnp.sqrt(squares)


def coefficients(left, right, scale, bias, first):
    logits = bias + scale * lax.dot_general(
        left, right, (((1,), (1,)), ((), ())), preferred_element_type=jnp.float32
    )
    coef = scale * jax.nn.sigmoid(logits)
    if first:
        row = lax.broadcasted_iota(jnp.int32, logits.shape, 0)
        col = lax.broadcasted_iota(jnp.int32, logits.shape, 1)
        coef = jnp.where(row == col, -scale * jax.nn.sigmoid(-logits), coef)
    return coef.astype(jnp.bfloat16)


def kernel(
    feats_hbm, proj_hbm, rest_hbm, text_hbm, scale_ref, bias_ref,
    gt_ref, head_ref,
    texts, images, feats, proj, rest, text, yv, grad, gyt, gx, htf, ht, ry, sf, sb, rz, total,
    load, t_send, t_recv, i_send, i_recv, f_send, f_recv, x_send, x_recv, y_send, y_recv,
    z_send, z_recv, a_send, a_recv, b_send, b_recv, c_send, c_recv,
):
    me = lax.axis_index("dp")
    k = lax.rem(me, 2)
    y = lax.rem(lax.div(me, 2), 4)
    z = lax.rem(lax.div(me, 8), 16)
    x = lax.div(me, 128)
    sib = me + 1 - 2 * k
    block = 2 * x + k

    def ring(delta):
        return lax.rem(me + (delta + N), N)

    def at(ax, az, ay, ak):
        return ((ax * 16 + az) * 4 + ay) * 2 + ak

    def xs(i):
        return lax.rem(x + (i + 4), 4)

    def ys(i):
        return lax.rem(y + (i + 4), 4)

    def zs(i):
        return lax.rem(z + (i + 16), 16)

    def remote(src, dst, send, recv, device):
        return pltpu.make_async_remote_copy(
            src_ref=src, dst_ref=dst, send_sem=send, recv_sem=recv,
            device_id=(device,), device_id_type=MESH,
        )

    def start(*args):
        copy = remote(*args)
        copy.start()
        return copy

    def landed(dst, recv):
        remote(dst, dst, t_send.at[0], recv, sib).wait_recv()

    loads = [
        pltpu.make_async_copy(text_hbm, text, load.at[0]),
        pltpu.make_async_copy(feats_hbm, feats.at[block], load.at[1]),
        pltpu.make_async_copy(proj_hbm, proj, load.at[2]),
        pltpu.make_async_copy(rest_hbm, rest, load.at[3]),
    ]
    for copy in loads:
        copy.start()

    barrier = pltpu.get_barrier_semaphore()
    partners = [ring(d) for d in (2, -2, 4, -4, 6, -6)] + [sib, ring(-7 + 14 * k)]
    partners += [at(xs(i), z, y, kk) for i in (1, 2, 3) for kk in (0, 1)]
    partners += [at(x, zs(i), y, k) for i in range(1, 16)]
    for device in partners:
        pl.semaphore_signal(barrier, inc=1, device_id=(device,), device_id_type=MESH)

    scale = scale_ref[0]
    bias = bias_ref[0]

    loads[0].wait()
    t_sq, t_unit = unit_rows(text[...].astype(jnp.float32))
    texts[0] = t_unit
    pl.semaphore_wait(barrier, len(partners))

    t_copies = []
    for j in (1, 2, 3):
        t_copies.append(start(texts.at[0], texts.at[2 * j], t_send.at[j], t_recv.at[2 * j], ring(2 * j)))

    def odd_text(j):
        slot = lax.rem(2 * j + 9 - 2 * k, 8)
        device = ring(1 + 6 * k) if j == 0 else sib
        return start(texts.at[2 * j], texts.at[slot], t_send.at[4 + j], t_recv.at[slot], device)

    t_copies.append(odd_text(0))
    loads[1].wait()
    f_copies = []
    for i in (1, 2, 3):
        f_copies.append(start(feats.at[block], feats.at[block], f_send.at[i], f_recv.at[i], at(xs(i), z, y, k)))
    f_copies.append(start(feats.at[block], feats.at[block], f_send.at[4], f_recv.at[4], sib))

    loads[2].wait()
    loads[3].wait()
    y_full = jnp.dot(feats[block], proj[...], preferred_element_type=jnp.float32)
    y_full = y_full + rest[...].astype(jnp.float32)
    yv[...] = y_full
    y_sq, image_unit = unit_rows(y_full)
    images[0] = image_unit

    def image_side(j):
        pair = texts[2 * j : 2 * j + 2].reshape(2 * B, D)
        coef = coefficients(images[0], pair, scale, bias, j == 0)
        part = jnp.dot(coef, pair, preferred_element_type=jnp.float32)
        if j == 0:
            grad[...] = part
        else:
            grad[...] += part

    def text_side(j):
        pair = images[2 * j : 2 * j + 2].reshape(2 * B, D)
        coef = coefficients(texts[0], pair, scale, bias, j == 0)
        part = jnp.dot(coef, pair, preferred_element_type=jnp.float32)
        if j == 0:
            grad[...] = part
        else:
            grad[...] += part

    for i in (1, 2, 3):
        there = feats.at[2 * xs(-i) + k]
        landed(there, f_recv.at[i])
        f_copies.append(start(there, there, f_send.at[4 + i], f_recv.at[4 + i], sib))

    for j in (1, 2, 3):
        landed(texts.at[2 * j], t_recv.at[2 * j])
        t_copies.append(odd_text(j))
        landed(texts.at[2 * j - 1], t_recv.at[2 * j - 1])
        image_side(j - 1)
    for copy in t_copies[:3]:
        copy.wait_send()

    i_copies = []
    for j in (1, 2, 3):
        i_copies.append(start(images.at[0], images.at[2 * j], i_send.at[j], i_recv.at[2 * j], ring(-2 * j)))

    def odd_image(j):
        slot = lax.rem(2 * j + 7 + 2 * k, 8)
        device = ring(-7 + 6 * k) if j == 0 else sib
        return start(images.at[2 * j], images.at[slot], i_send.at[4 + j], i_recv.at[slot], device)

    i_copies.append(odd_image(0))

    landed(texts.at[7], t_recv.at[7])
    image_side(3)
    for copy in t_copies[3:]:
        copy.wait_send()

    grad_y = back_norm(yv[...], y_sq, grad[...]).astype(jnp.bfloat16)
    gyt[...] = jnp.transpose(grad_y.astype(jnp.float32)).astype(jnp.bfloat16).reshape(8, ROWS, B)

    x_copies = []
    for i in range(4):
        for kk in (0, 1):
            if i or kk:
                other = lax.rem(k + kk, 2)
                n = 2 * i + kk - 1
                x_copies.append(
                    start(gyt.at[2 * xs(i) + other], gx.at[block], x_send.at[n], x_recv.at[n], at(xs(i), z, y, other))
                )
    gx[block] = gyt[block]
    for i in range(4):
        there = feats.at[2 * xs(-i) + 1 - k]
        landed(there, f_recv.at[4 + i])
    for i in range(4):
        for kk in (0, 1):
            if i or kk:
                n = 2 * i + kk - 1
                landed(gx.at[2 * xs(-i) + lax.rem(k + kk, 2)], x_recv.at[n])
    left = jnp.concatenate([gx[b] for b in range(8)], axis=1)
    head = jnp.dot(left, feats[...].reshape(8 * B, F), preferred_element_type=jnp.float32)
    for i in range(9):
        for j in range(5):
            tile = head[16 * i : 16 * i + 16, 128 * j : 128 * j + 128]
            htf[5 * i + j] = tile
            ht[5 * i + j] = tile.astype(jnp.bfloat16)
    for n in range(TILES, PAD):
        htf[n] = jnp.zeros((16, 128), jnp.float32)
        ht[n] = jnp.zeros((16, 128), jnp.bfloat16)

    y_copies = []
    for i in (1, 2, 3):
        y_copies.append(
            start(ht.at[pl.ds(OWN * ys(i), OWN)], ry.at[i - 1], y_send.at[i - 1], y_recv.at[i - 1], at(x, z, ys(i), k))
        )
    for i in (1, 2, 3):
        landed(ry.at[i - 1], y_recv.at[i - 1])
    mine = htf[pl.ds(OWN * y, OWN)]
    for i in (0, 1, 2):
        mine = mine + ry[i].astype(jnp.float32)
    sf[...] = mine
    sb[...] = mine.astype(jnp.bfloat16)

    def z_copy(i):
        return remote(sb.at[zs(i)], rz.at[i - 1], z_send.at[i - 1], z_recv.at[i - 1], at(x, zs(i), y, k))

    for i in range(1, 16):
        @pl.when(zs(i) < OWN)
        def _():
            z_copy(i).start()

    for j in (1, 2, 3):
        landed(images.at[2 * j], i_recv.at[2 * j])
        i_copies.append(odd_image(j))
        landed(images.at[2 * j - 1], i_recv.at[2 * j - 1])
        text_side(j - 1)

    @pl.when(z < OWN)
    def _():
        for i in range(1, 16):
            landed(rz.at[i - 1], z_recv.at[i - 1])
        tile = sf[z]
        for i in range(15):
            tile = tile + rz[i].astype(jnp.float32)
        total[block, OWN * y + z] = (tile / N).astype(jnp.bfloat16)

    def a_copy(i):
        there = total.at[block, OWN * y + z]
        return remote(there, there, a_send.at[i - 1], a_recv.at[i - 1], at(x, zs(i), y, k))

    @pl.when(z < OWN)
    def _():
        for i in range(1, 16):
            a_copy(i).start()

    landed(images.at[7], i_recv.at[7])
    text_side(3)
    gt_ref[...] = back_norm(text[...].astype(jnp.float32), t_sq, grad[...]).astype(jnp.bfloat16)

    for i in range(1, 16):
        @pl.when(zs(-i) < OWN)
        def _():
            landed(total.at[block, OWN * y + zs(-i)], a_recv.at[i - 1])

    b_copies = []
    for i in (1, 2, 3):
        there = total.at[block, pl.ds(OWN * y, OWN)]
        b_copies.append(start(there, there, b_send.at[i - 1], b_recv.at[i - 1], at(x, z, ys(i), k)))
    for i in (1, 2, 3):
        landed(total.at[block, pl.ds(OWN * ys(-i), OWN)], b_recv.at[i - 1])

    c_copies = []
    there = total.at[block]
    for i in (1, 2, 3):
        c_copies.append(start(there, there, c_send.at[i], c_recv.at[i], at(xs(i), z, y, k)))
    c_copies.append(start(there, there, c_send.at[4], c_recv.at[4], sib))
    for i in (1, 2, 3):
        there = total.at[2 * xs(-i) + k]
        landed(there, c_recv.at[i])
        c_copies.append(start(there, there, c_send.at[4 + i], c_recv.at[4 + i], sib))
    for i in range(4):
        landed(total.at[2 * xs(-i) + 1 - k], c_recv.at[4 + i])
    for b in range(8):
        for i in range(9):
            for j in range(5):
                head_ref[ROWS * b + 16 * i : ROWS * b + 16 * i + 16, 128 * j : 128 * j + 128] = total[b, 5 * i + j]

    for copy in f_copies + i_copies + x_copies + y_copies + b_copies + c_copies:
        copy.wait_send()
    for i in range(1, 16):
        @pl.when(zs(i) < OWN)
        def _():
            z_copy(i).wait_send()

    @pl.when(z < OWN)
    def _():
        for i in range(1, 16):
            a_copy(i).wait_send()


def on_device(image_feats, proj_head, rest_part, text_embed, logit_scale, logit_bias):
    any_spec = pl.BlockSpec(memory_space=pl.ANY)
    vmem = pl.BlockSpec(memory_space=pltpu.VMEM)
    smem = pl.BlockSpec(memory_space=pltpu.SMEM)
    bf16, f32 = jnp.bfloat16, jnp.float32
    sems = lambda n: pltpu.SemaphoreType.DMA((n,))
    grad_text, head = pl.pallas_call(
        kernel,
        out_shape=(jax.ShapeDtypeStruct((B, D), bf16), jax.ShapeDtypeStruct((D, F), bf16)),
        in_specs=[any_spec] * 4 + [smem] * 2,
        out_specs=(vmem, vmem),
        scratch_shapes=[
            pltpu.VMEM((8, B, D), bf16),
            pltpu.VMEM((8, B, D), bf16),
            pltpu.VMEM((8, B, F), bf16),
            pltpu.VMEM((F, D), bf16),
            pltpu.VMEM((B, D), bf16),
            pltpu.VMEM((B, D), bf16),
            pltpu.VMEM((B, D), f32),
            pltpu.VMEM((B, D), f32),
            pltpu.VMEM((8, ROWS, B), bf16),
            pltpu.VMEM((8, ROWS, B), bf16),
            pltpu.VMEM((PAD, 16, 128), f32),
            pltpu.VMEM((PAD, 16, 128), bf16),
            pltpu.VMEM((3, OWN, 16, 128), bf16),
            pltpu.VMEM((OWN, 16, 128), f32),
            pltpu.VMEM((OWN, 16, 128), bf16),
            pltpu.VMEM((15, 16, 128), bf16),
            pltpu.VMEM((8, PAD, 16, 128), bf16),
            sems(4), sems(8), sems(8), sems(8), sems(8), sems(8), sems(8), sems(7), sems(7), sems(3), sems(3),
            sems(15), sems(15), sems(15), sems(15), sems(3), sems(3), sems(8), sems(8),
        ],
        compiler_params=pltpu.CompilerParams(
            collective_id=0, has_side_effects=True, vmem_limit_bytes=48 * 2**20
        ),
    )(image_feats, proj_head, rest_part, text_embed, logit_scale, logit_bias)
    return grad_text, head.T


def solution(mesh):
    placed = (P("dp", None), P(), P("dp", None), P("dp", None), P(), P())
    return jax.shard_map(
        on_device, mesh=mesh, in_specs=placed, out_specs=(P("dp", None), P()), check_vma=False
    )
```

time: 610 us -> 110 us (0.18)
  waiting for transfers between devices: 536 us -> 0 us
  Pallas kernels: 0 us -> 99.4 us
  starting transfers between devices: 35.6 us -> 0 us
  between operations: 15.8 us -> 1.94 us
  matrix products: 9.94 us -> 0 us
  other arithmetic: 8.86 us -> 0 us
    psum x1 -> x0, waiting for transfers between devices: 440 us -> none  [on_device(): head_total = lax.psum(head_local, 'dp')]
    pallas_call x0 -> x1, Pallas kernels: none -> 99.4 us  [on_device(): pl.pallas_call(kernel, out_shape=(jax.ShapeDtypeStruct((B, D), bf16), jax...]
    ppermute x15 -> x0, waiting for transfers between devices: 96.6 us -> none  [from_behind(): return lax.ppermute(block, axis, route)]
    ppermute x15 -> x0, starting transfers between devices: 35.6 us -> none  [from_behind(): return lax.ppermute(block, axis, route)]
    dot_general x26 -> x0, matrix products: 9.94 us -> none  [the longest x9 4.36 us: transposed(): lax.dot_general(coef, block, (((0,), (0,)), ((), ())), preferred_element_...]
  transfers between devices with their start and end apart: 16 -> 0, of which waited for: 11 -> 0; matrix products, arithmetic and copies ran while one was open for 3% -> 0% of each run, Pallas kernels for 0% -> 0%
where the time goes in v1:
time: 110 us; the launch traced here: 108 us
  Pallas kernels  99.4 us (90%)
  local copies, waits for them, and re-layouts  7 us (6%)
  between operations  1.94 us (2%)
    pallas_call x1, Pallas kernels, on_device(): pl.pallas_call(kernel, out_shape=(jax.ShapeDtypeStruct((B, D), bf16), jax...  99.4 us
    unnamed x10, local copies, waits for them, and re-layouts  7 us

profile of v1, /device:TPU:1, one launch (start us, length us, event | category | flops | bytes accessed | tf_op | source)
XLA Modules:
  0.0 108.3 jit_solution(923200169779172384)
XLA Ops:
  1.9 0.0 copy-start
  1.9 1.4 %copy-done = bf16[640,1152]{1,0:T(8,128)(2,1)S(1)} copy-done((bf16[640,1152]{1,0:T(8,128)(2,1)S(1)}, bf16[640,1152]{1,0:T(8,128)(2,1)}, u32[]{:S(2)}) %copy-start) | copy-done | bytes 1474584
  3.3 0.0 copy-start.1
  3.3 1.0 copy-done.1
  4.3 0.0 copy-start.2
  4.3 1.0 copy-done.2
  5.2 0.0 copy-start.3
  5.2 0.9 copy-done.3
  6.1 99.4 %shard_map.77 = (bf16[128,1152]{1,0:T(8,128)(2,1)S(1)}, bf16[1152,640]{1,0:T(8,128)(2,1)S(1)}) custom-call(bf16[128,640]{1,0:T(8,128)(2,1)S(1)} %copy-done.3, bf16[640,1152]{1,0:T(8,128)(2,1)S(1)} %copy-done, bf16[128,1152]{1,0:T(8,128)(2,1)S(1)} %copy-done.1, bf16[128,1152]{1,0:T(8,128)(2,1)S(1)} %copy-done.2, f32[1]{0:T(128)S(6)} %copy.10.scale_ref, ...), custom_call_target="tpu_custom_call" | custom-call | tf_op jit(solution)/shard_map/pallas_call | solution.py:308
  105.5 2.1 %copy.8 = bf16[640,1152]{1,0:T(8,128)(2,1)} copy(bf16[640,1152]{0,1:T(8,128)(2,1)S(1)} %bitcast.1) | data formatting | bytes 2949120
  107.6 0.7 copy.12
Async XLA Ops:
  1.9 1.4 %copy-start = (bf16[640,1152]{1,0:T(8,128)(2,1)S(1)}, bf16[640,1152]{1,0:T(8,128)(2,1)}, u32[]{:S(2)}) copy-start(bf16[640,1152]{1,0:T(8,128)(2,1)} %proj_hbm.1) | copy-start | bytes 4423684
  3.3 1.0 copy-start.1
  4.3 1.0 copy-start.2
  5.2 0.9 copy-start.3

commit v2 on v1

v2 whole, which is shorter than its diff:
```python
import jax
import jax.numpy as jnp
from jax import lax
from jax.experimental import pallas as pl
from jax.experimental.pallas import tpu as pltpu
from jax.sharding import PartitionSpec as P

D = 1152
F = 640
B = 128
N = 512
MESH = pl.DeviceIdType.MESH
ROWS = 144
TILES = 45
OWN = 12
PARTS = 3
HALF = B // 2


def unit_rows(values):
    squares = jnp.sum(values * values, axis=-1, keepdims=True) + 1e-06
    return squares, (values / jnp.sqrt(squares)).astype(jnp.bfloat16)


def back_norm(values, squares, grads):
    inner = jnp.sum(values * grads, axis=-1, keepdims=True)
    return (grads - values * (inner / squares)) / jnp.sqrt(squares)


def coefficients(left, right, scale, bias, first):
    logits = bias + scale * lax.dot_general(
        left, right, (((1,), (1,)), ((), ())), preferred_element_type=jnp.float32
    )
    coef = scale * jax.nn.sigmoid(logits)
    if first:
        row = lax.broadcasted_iota(jnp.int32, logits.shape, 0)
        col = lax.broadcasted_iota(jnp.int32, logits.shape, 1)
        coef = jnp.where(row == col, -scale * jax.nn.sigmoid(-logits), coef)
    return coef.astype(jnp.bfloat16)


def kernel(
    feats_hbm, proj_hbm, rest_hbm, text_hbm, scale_ref, bias_ref,
    gt_ref, head_ref,
    texts, images, feats, proj, rest, text, yv, grad, gyt, gx, htf, ht, ry, sf, sb, rz, total, headt,
    reach, load, t_send, t_recv, i_send, i_recv, f_send, f_recv, x_send, x_recv, y_send, y_recv,
    z_send, z_recv, a_send, a_recv, b_send, b_recv, c_send, c_recv,
):
    me = lax.axis_index("dp")
    k = lax.rem(me, 2)
    y = lax.rem(lax.div(me, 2), 4)
    z = lax.rem(lax.div(me, 8), 16)
    x = lax.div(me, 128)
    sib = me + 1 - 2 * k
    block = 2 * x + k

    def ring(delta):
        return lax.rem(me + (delta + N), N)

    def at(ax, az, ay, ak):
        return ((ax * 16 + az) * 4 + ay) * 2 + ak

    def xs(i):
        return lax.rem(x + (i + 4), 4)

    def ys(i):
        return lax.rem(y + (i + 4), 4)

    def zs(i):
        return lax.rem(z + (i + 16), 16)

    def remote(src, dst, send, recv, device):
        return pltpu.make_async_remote_copy(
            src_ref=src, dst_ref=dst, send_sem=send, recv_sem=recv,
            device_id=(device,), device_id_type=MESH,
        )

    def start(*args):
        copy = remote(*args)
        copy.start()
        return copy

    def landed(dst, recv):
        remote(dst, dst, t_send.at[0], recv, sib).wait_recv()

    loads = [
        pltpu.make_async_copy(text_hbm, text, load.at[0]),
        pltpu.make_async_copy(feats_hbm, feats.at[block], load.at[1]),
        pltpu.make_async_copy(proj_hbm, proj, load.at[2]),
        pltpu.make_async_copy(rest_hbm, rest, load.at[3]),
    ]
    for copy in loads:
        copy.start()

    plane = [(2, 2), (2, 1), (2, 3), (1, 2), (3, 2), (1, 1), (1, 3), (3, 1), (3, 3), (0, 2), (2, 0), (1, 0), (3, 0), (0, 1), (0, 3)]
    barrier = pltpu.get_barrier_semaphore()
    partners = [ring(d) for d in (2, -2, 6, -6, 8, -8)] + [sib, ring(-7 + 14 * k)]
    partners += [at(xs(i), z, y, 1 - k) for i in (1, 2, 3)]
    partners += [at(xs(i), z, ys(j), k) for i, j in plane]
    partners += [at(x, zs(i), y, k) for i in (1, -1)]
    for device in partners:
        pl.semaphore_signal(barrier, inc=1, device_id=(device,), device_id_type=MESH)

    def tell(n, distance):
        for i in (distance, -distance):
            pl.semaphore_signal(reach.at[n], inc=1, device_id=(at(x, zs(i), y, k),), device_id_type=MESH)

    scale = scale_ref[0]
    bias = bias_ref[0]

    loads[0].wait()
    t_sq, t_unit = unit_rows(text[...].astype(jnp.float32))
    texts[0] = t_unit
    pl.semaphore_wait(barrier, len(partners))
    tell(0, 1)

    low, high = pl.ds(0, HALF), pl.ds(HALF, HALF)
    halves = (low, high)
    at_end = lax.div(y, 3)
    at_start = lax.div(3 - y, 3)
    inner = at_end + at_start == 0
    t_copies = []
    for h, rows in enumerate(halves):
        slot = 2 + 6 * at_end
        t_copies.append(start(texts.at[0, rows], texts.at[slot, rows], t_send.at[h], t_recv.at[slot, h], ring(2 - 8 * at_end)))
        t_copies.append(start(texts.at[0, rows], texts.at[6, rows], t_send.at[2 + h], t_recv.at[6, h], ring(6)))

    def odd_text(j):
        slot = lax.rem(2 * j + 9 - 2 * k, 8)
        device = ring(1 + 6 * k) if j == 0 else sib
        return start(texts.at[2 * j], texts.at[slot], t_send.at[4 + j], t_recv.at[slot, 0], device)

    t_copies.append(odd_text(0))

    def t_edge(h):
        return remote(texts.at[8, halves[h]], texts.at[2, halves[h]], t_send.at[8 + h], t_recv.at[2, h], ring(8))

    def t_inner(h, slot, n, delta):
        rows = halves[h]
        return remote(texts.at[slot, rows], texts.at[4, rows], t_send.at[n + h], t_recv.at[4, h], ring(delta))

    loads[1].wait()
    loads[2].wait()
    loads[3].wait()
    y_full = jnp.dot(feats[block], proj[...], preferred_element_type=jnp.float32)
    y_full = y_full + rest[...].astype(jnp.float32)
    yv[...] = y_full
    y_sq, image_unit = unit_rows(y_full)
    images[0] = image_unit
    pl.semaphore_wait(reach.at[0], 2)
    tell(1, 2)

    def pair_of(held, a, b):
        return jnp.concatenate([held[a], held[b]], axis=0)

    def gather_grad(unit, pair, first):
        coef = coefficients(unit, pair, scale, bias, first)
        part = jnp.dot(coef, pair, preferred_element_type=jnp.float32)
        if first:
            grad[...] = part
        else:
            grad[...] += part

    for h, rows in enumerate(halves):
        @pl.when(y == 0)
        def _():
            landed(texts.at[8, rows], t_recv.at[8, h])
            t_edge(h).start()

        landed(texts.at[6, rows], t_recv.at[6, h])

        @pl.when(y > 0)
        def _():
            landed(texts.at[2, rows], t_recv.at[2, h])

        @pl.when(inner)
        def _():
            t_inner(h, 6, 10, -2).start()
            t_inner(h, 2, 12, 2).start()

    t_copies.append(odd_text(3))
    pl.semaphore_wait(reach.at[1], 2)
    tell(2, 4)

    f_copies = []
    for i in (2, 1, 3):
        f_copies.append(start(feats.at[block], feats.at[block], f_send.at[i], f_recv.at[i], at(xs(i), z, y, k)))
    f_copies.append(start(feats.at[block], feats.at[block], f_send.at[4], f_recv.at[4], sib))

    landed(texts.at[1], t_recv.at[1, 0])
    gather_grad(images[0], pair_of(texts, 0, 1), True)
    landed(texts.at[7], t_recv.at[7, 0])
    gather_grad(images[0], pair_of(texts, 6, 7), False)

    @pl.when(y == 0)
    def _():
        for h, rows in enumerate(halves):
            landed(texts.at[2, rows], t_recv.at[2, h])

    t_copies.append(odd_text(1))
    landed(texts.at[5 - 2 * k], t_recv.at[5 - 2 * k, 0])
    gather_grad(images[0], pair_of(texts, 2, 5 - 2 * k), False)
    for h, rows in enumerate(halves):
        landed(texts.at[4, rows], t_recv.at[4, h])
    t_copies.append(odd_text(2))
    landed(texts.at[3 + 2 * k], t_recv.at[3 + 2 * k, 0])
    gather_grad(images[0], pair_of(texts, 4, 3 + 2 * k), False)

    grad_y = back_norm(yv[...], y_sq, grad[...]).astype(jnp.bfloat16)
    gyt[...] = jnp.transpose(grad_y.astype(jnp.float32)).astype(jnp.bfloat16).reshape(8, ROWS, B)

    x_copies = []
    across = [(2, 0), (2, 1), (1, 0), (1, 1), (3, 0), (3, 1), (0, 1)]
    for n, (i, kk) in enumerate(across):
        other = lax.rem(k + kk, 2)
        x_copies.append(
            start(gyt.at[2 * xs(i) + other], gx.at[block], x_send.at[n], x_recv.at[n], at(xs(i), z, y, other))
        )
    gx[block] = gyt[block]
    for i in (1, 3, 2):
        there = feats.at[2 * xs(-i) + k]
        landed(there, f_recv.at[i])
        f_copies.append(start(there, there, f_send.at[4 + i], f_recv.at[4 + i], sib))
    for i in range(4):
        landed(feats.at[2 * xs(-i) + 1 - k], f_recv.at[4 + i])
    for n, (i, kk) in enumerate(across):
        landed(gx.at[2 * xs(-i) + lax.rem(k + kk, 2)], x_recv.at[n])
    left = jnp.concatenate([gx[b] for b in range(8)], axis=1)
    head = jnp.dot(left, feats[...].reshape(8 * B, F), preferred_element_type=jnp.float32)
    for n in range(PARTS * 16):
        i, j = n // 5, n % 5
        if n < TILES:
            tile = head[16 * i : 16 * i + 16, 128 * j : 128 * j + 128]
        else:
            tile = jnp.zeros((16, 128), jnp.float32)
        htf[n // 16, n % 16] = tile
        ht[n // 16, n % 16] = tile.astype(jnp.bfloat16)

    y_copies = []
    for i in (2, 1, 3):
        y_copies.append(
            start(ht.at[:, pl.ds(4 * ys(i), 4)], ry.at[i - 1], y_send.at[i - 1], y_recv.at[i - 1], at(x, z, ys(i), k))
        )
    for i in (1, 3, 2):
        landed(ry.at[i - 1], y_recv.at[i - 1])
    mine = htf[:, pl.ds(4 * y, 4)]
    for i in (0, 1, 2):
        mine = mine + ry[i].astype(jnp.float32)
    mine = mine.reshape(OWN, 16, 128)
    sf[...] = mine
    sb[...] = mine.astype(jnp.bfloat16)

    far_first = (8, 7, 9, 6, 10, 5, 11, 4, 12, 3, 13, 2, 14, 1, 15)
    w = lax.rem(z + 12, 16)

    def ws(i):
        return lax.rem(w + (i + 16), 16)

    def z_copy(i):
        return remote(sb.at[ws(i)], rz.at[i - 1], z_send.at[i - 1], z_recv.at[i - 1], at(x, zs(i), y, k))

    pl.semaphore_wait(reach.at[2], 2)
    for i in far_first:
        @pl.when(ws(i) < OWN)
        def _():
            z_copy(i).start()

    i_copies = []
    for h, rows in enumerate(halves):
        slot = 2 + 6 * at_start
        i_copies.append(start(images.at[0, rows], images.at[slot, rows], i_send.at[h], i_recv.at[slot, h], ring(8 * at_start - 2)))
        i_copies.append(start(images.at[0, rows], images.at[6, rows], i_send.at[2 + h], i_recv.at[6, h], ring(-6)))

    def odd_image(j):
        slot = lax.rem(2 * j + 7 + 2 * k, 8)
        device = ring(-7 + 6 * k) if j == 0 else sib
        return start(images.at[2 * j], images.at[slot], i_send.at[4 + j], i_recv.at[slot, 0], device)

    i_copies.append(odd_image(0))

    def i_edge(h):
        return remote(images.at[8, halves[h]], images.at[2, halves[h]], i_send.at[8 + h], i_recv.at[2, h], ring(-8))

    def i_inner(h, slot, n, delta):
        rows = halves[h]
        return remote(images.at[slot, rows], images.at[4, rows], i_send.at[n + h], i_recv.at[4, h], ring(delta))

    def pass_on_images(h):
        rows = halves[h]

        @pl.when(y == 3)
        def _():
            landed(images.at[8, rows], i_recv.at[8, h])
            i_edge(h).start()

        landed(images.at[6, rows], i_recv.at[6, h])

        @pl.when(y < 3)
        def _():
            landed(images.at[2, rows], i_recv.at[2, h])

        @pl.when(inner)
        def _():
            i_inner(h, 6, 10, 2).start()
            i_inner(h, 2, 12, -2).start()

    pass_on_images(0)

    part = lax.div(w, 4)
    own = total.at[block, part, 4 * y + lax.rem(w, 4)]

    @pl.when(w < OWN)
    def _():
        for i in range(1, 16):
            landed(rz.at[i - 1], z_recv.at[i - 1])
        tile = sf[w]
        for i in range(15):
            tile = tile + rz[i].astype(jnp.float32)
        own[...] = (tile / N).astype(jnp.bfloat16)

    def a_copy(i):
        return remote(own, own, a_send.at[i - 1], a_recv.at[w], at(x, zs(i), y, k))

    @pl.when(w < OWN)
    def _():
        for i in far_first:
            a_copy(i).start()

    pass_on_images(1)
    i_copies.append(odd_image(3))
    landed(images.at[1], i_recv.at[1, 0])
    gather_grad(texts[0], pair_of(images, 0, 1), True)
    landed(images.at[7], i_recv.at[7, 0])
    gather_grad(texts[0], pair_of(images, 6, 7), False)

    first = part - lax.div(w, 12)
    last = lax.rem(lax.div(w, 6) + 2, 3)
    b_copies = []
    parts = (first, 3 - first - last, last)
    for n, q in enumerate(parts):
        for r in range(4):
            owner = 4 * q + r

            @pl.when(owner != w)
            def _():
                landed(total.at[block, q, 4 * y + r], a_recv.at[owner])

        there = total.at[block, q, pl.ds(4 * y, 4)]
        for m, (i, j) in enumerate(plane):
            b_copies.append(start(there, there, b_send.at[n, m], b_recv.at[n, m], at(xs(i), z, ys(j), k)))

    @pl.when(y == 3)
    def _():
        for h, rows in enumerate(halves):
            landed(images.at[2, rows], i_recv.at[2, h])

    i_copies.append(odd_image(1))
    for h, rows in enumerate(halves):
        landed(images.at[4, rows], i_recv.at[4, h])
    i_copies.append(odd_image(2))
    landed(images.at[3 + 2 * k], i_recv.at[3 + 2 * k, 0])
    gather_grad(texts[0], pair_of(images, 2, 3 + 2 * k), False)
    landed(images.at[5 - 2 * k], i_recv.at[5 - 2 * k, 0])
    gather_grad(texts[0], pair_of(images, 4, 5 - 2 * k), False)
    gt_ref[...] = back_norm(text[...].astype(jnp.float32), t_sq, grad[...]).astype(jnp.bfloat16)

    c_copies = []
    for n, q in enumerate(parts):
        for i in range(4):
            for m, (pi, pj) in enumerate(plane):
                if pi == i:
                    landed(total.at[2 * xs(-pi) + k, q, pl.ds(4 * ys(-pj), 4)], b_recv.at[n, m])
            there = total.at[2 * xs(-i) + k, q]
            c_copies.append(start(there, there, c_send.at[n, i], c_recv.at[n, i], sib))
    for n, q in enumerate(parts):
        for i in range(4):
            landed(total.at[2 * xs(-i) + 1 - k, q], c_recv.at[n, i])
    for b in range(8):
        for n in range(TILES):
            i, j = n // 5, n % 5
            headt[ROWS * b + 16 * i : ROWS * b + 16 * i + 16, 128 * j : 128 * j + 128] = total[b, n // 16, n % 16]

    for i in range(9):
        for j in range(5):
            block_t = headt[128 * i : 128 * i + 128, 128 * j : 128 * j + 128].astype(jnp.float32)
            head_ref[128 * j : 128 * j + 128, 128 * i : 128 * i + 128] = jnp.transpose(block_t).astype(jnp.bfloat16)

    for copy in t_copies + f_copies + i_copies + x_copies + y_copies + b_copies + c_copies:
        copy.wait_send()
    for i in far_first:
        @pl.when(ws(i) < OWN)
        def _():
            z_copy(i).wait_send()

    @pl.when(y == 0)
    def _():
        for h in (0, 1):
            t_edge(h).wait_send()

    @pl.when(y == 3)
    def _():
        for h in (0, 1):
            i_edge(h).wait_send()

    @pl.when(inner)
    def _():
        for h in (0, 1):
            t_inner(h, 6, 10, -2).wait_send()
            t_inner(h, 2, 12, 2).wait_send()
            i_inner(h, 6, 10, 2).wait_send()
            i_inner(h, 2, 12, -2).wait_send()

    @pl.when(w < OWN)
    def _():
        for i in far_first:
            a_copy(i).wait_send()


def on_device(image_feats, proj_head, rest_part, text_embed, logit_scale, logit_bias):
    any_spec = pl.BlockSpec(memory_space=pl.ANY)
    vmem = pl.BlockSpec(memory_space=pltpu.VMEM)
    smem = pl.BlockSpec(memory_space=pltpu.SMEM)
    bf16, f32 = jnp.bfloat16, jnp.float32
    sems = lambda *n: pltpu.SemaphoreType.DMA(n)
    grad_text, head = pl.pallas_call(
        kernel,
        out_shape=(jax.ShapeDtypeStruct((B, D), bf16), jax.ShapeDtypeStruct((F, D), bf16)),
        in_specs=[any_spec] * 4 + [smem] * 2,
        out_specs=(vmem, vmem),
        scratch_shapes=[
            pltpu.VMEM((9, B, D), bf16),
            pltpu.VMEM((9, B, D), bf16),
            pltpu.VMEM((8, B, F), bf16),
            pltpu.VMEM((F, D), bf16),
            pltpu.VMEM((B, D), bf16),
            pltpu.VMEM((B, D), bf16),
            pltpu.VMEM((B, D), f32),
            pltpu.VMEM((B, D), f32),
            pltpu.VMEM((8, ROWS, B), bf16),
            pltpu.VMEM((8, ROWS, B), bf16),
            pltpu.VMEM((PARTS, 16, 16, 128), f32),
            pltpu.VMEM((PARTS, 16, 16, 128), bf16),
            pltpu.VMEM((3, PARTS, 4, 16, 128), bf16),
            pltpu.VMEM((OWN, 16, 128), f32),
            pltpu.VMEM((OWN, 16, 128), bf16),
            pltpu.VMEM((15, 16, 128), bf16),
            pltpu.VMEM((8, PARTS, 16, 16, 128), bf16),
            pltpu.VMEM((D, F), bf16),
            pltpu.SemaphoreType.REGULAR((3,)), sems(4), sems(14), sems(9, 2), sems(14), sems(9, 2), sems(8), sems(8), sems(7), sems(7), sems(3), sems(3),
            sems(15), sems(15), sems(15), sems(12), sems(3, 15), sems(3, 15), sems(3, 4), sems(3, 4),
        ],
        compiler_params=pltpu.CompilerParams(
            collective_id=0, has_side_effects=True, vmem_limit_bytes=60 * 2**20
        ),
    )(image_feats, proj_head, rest_part, text_embed, logit_scale, logit_bias)
    return grad_text, head


def solution(mesh):
    placed = (P("dp", None), P(), P("dp", None), P("dp", None), P(), P())
    return jax.shard_map(
        on_device, mesh=mesh, in_specs=placed, out_specs=(P("dp", None), P()), check_vma=False
    )
```

time: 110 us -> 83.2 us (0.76); the launches traced: 108 us -> 83 us
  Pallas kernels: 99.4 us -> 76.8 us
  local copies, waits for them, and re-layouts: 7 us -> 4.29 us
    pallas_call x1, Pallas kernels: 99.4 us -> 76.8 us  [on_device(): pl.pallas_call(kernel, out_shape=(jax.ShapeDtypeStruct((B, D), bf16), jax...]
    unnamed x10 -> x2, local copies, waits for them, and re-layouts: 7 us -> 4.29 us
where the time goes in v2:
time: 83.2 us; the launch traced here: 83 us
  Pallas kernels  76.8 us (92%)
  local copies, waits for them, and re-layouts  4.29 us (5%)
  between operations  1.93 us (2%)
    pallas_call x1, Pallas kernels, on_device(): pl.pallas_call(kernel, out_shape=(jax.ShapeDtypeStruct((B, D), bf16), jax...  76.8 us
    unnamed x2, local copies, waits for them, and re-layouts  4.29 us

profile of v2, /device:TPU:1, one launch (start us, length us, event | category | flops | bytes accessed | tf_op | source)
XLA Modules:
  0.0 83.0 jit_solution(17529364764542088435)
XLA Ops:
  1.9 76.8 %shard_map.77 = (bf16[128,1152]{1,0:T(8,128)(2,1)}, bf16[640,1152]{1,0:T(8,128)(2,1)}) custom-call(bf16[128,640]{1,0:T(8,128)(2,1)} %feats_hbm.1, bf16[640,1152]{1,0:T(8,128)(2,1)} %proj_hbm.1, bf16[128,1152]{1,0:T(8,128)(2,1)} %rest_hbm.1, bf16[128,1152]{1,0:T(8,128)(2,1)} %text_hbm.1, f32[1]{0:T(128)S(6)} %copy.10.scale_ref, f32[1]{0:T(128)S(6)} %copy.11.bias_ref), custom_call_target="tpu_custom_call" | custom-call | tf_op jit(solution)/shard_map/pallas_call | solution.py:425
  78.7 1.7 %copy.12 = bf16[128,1152]{1,0:T(8,128)(2,1)} copy(bf16[128,1152]{1,0:T(8,128)(2,1)} %get-tuple-element.4) | data formatting | bytes 589824
  80.4 2.6 %copy.13 = bf16[640,1152]{1,0:T(8,128)(2,1)} copy(bf16[640,1152]{1,0:T(8,128)(2,1)} %get-tuple-element.5) | data formatting | bytes 2949120

commit v3 on v2

--- a/solution.py
+++ b/solution.py
@@ -96,7 +96,7 @@
     barrier = pltpu.get_barrier_semaphore()
     partners = [ring(d) for d in (2, -2, 6, -6, 8, -8)] + [sib, ring(-7 + 14 * k)]
     partners += [at(xs(i), z, y, 1 - k) for i in (1, 2, 3)]
-    partners += [at(xs(i), z, ys(j), k) for i, j in plane]
+    partners += [at(xs(i), z, ys(j), k) for i, j in plane if i == 0 or j == 0]
     partners += [at(x, zs(i), y, k) for i in (1, -1)]
     for device in partners:
         pl.semaphore_signal(barrier, inc=1, device_id=(device,), device_id_type=MESH)
@@ -182,6 +182,28 @@
     pl.semaphore_wait(reach.at[1], 2)
     tell(2, 4)
 
+    def image_copy(n):
+        if n == 0:
+            slot = 2 + 6 * at_start
+            return remote(images.at[0], images.at[slot], i_send.at[0], i_recv.at[slot], ring(8 * at_start - 2))
+        return remote(images.at[0], images.at[6], i_send.at[1], i_recv.at[6], ring(-6))
+
+    def odd_image(j):
+        slot = lax.rem(2 * j + 7 + 2 * k, 8)
+        device = ring(-7 + 6 * k) if j == 0 else sib
+        return start(images.at[2 * j], images.at[slot], i_send.at[4 + j], i_recv.at[slot], device)
+
+    image_edge = remote(images.at[8], images.at[2], i_send.at[2], i_recv.at[2], ring(-8))
+    image_inner = [
+        remote(images.at[6], images.at[4], i_send.at[3], i_recv.at[4], ring(2)),
+        remote(images.at[2], images.at[4], i_send.at[8], i_recv.at[4], ring(-2)),
+    ]
+
+    @pl.when(jnp.logical_not(inner))
+    def _():
+        image_copy(0).start()
+        image_copy(1).start()
+
     f_copies = []
     for i in (2, 1, 3):
         f_copies.append(start(feats.at[block], feats.at[block], f_send.at[i], f_recv.at[i], at(xs(i), z, y, k)))
@@ -216,6 +238,14 @@
         x_copies.append(
             start(gyt.at[2 * xs(i) + other], gx.at[block], x_send.at[n], x_recv.at[n], at(xs(i), z, y, other))
         )
+    @pl.when(inner)
+    def _():
+        image_copy(0).start()
+
+    @pl.when(jnp.logical_and(inner, z > 0))
+    def _():
+        image_copy(1).start()
+
     gx[block] = gyt[block]
     for i in (1, 3, 2):
         there = feats.at[2 * xs(-i) + k]
@@ -241,6 +271,11 @@
         y_copies.append(
             start(ht.at[:, pl.ds(4 * ys(i), 4)], ry.at[i - 1], y_send.at[i - 1], y_recv.at[i - 1], at(x, z, ys(i), k))
         )
+    @pl.when(y == 3)
+    def _():
+        landed(images.at[8], i_recv.at[8])
+        image_edge.start()
+
     for i in (1, 3, 2):
         landed(ry.at[i - 1], y_recv.at[i - 1])
     mine = htf[:, pl.ds(4 * y, 4)]
@@ -265,46 +300,19 @@
         def _():
             z_copy(i).start()
 
-    i_copies = []
-    for h, rows in enumerate(halves):
-        slot = 2 + 6 * at_start
-        i_copies.append(start(images.at[0, rows], images.at[slot, rows], i_send.at[h], i_recv.at[slot, h], ring(8 * at_start - 2)))
-        i_copies.append(start(images.at[0, rows], images.at[6, rows], i_send.at[2 + h], i_recv.at[6, h], ring(-6)))
-
-    def odd_image(j):
-        slot = lax.rem(2 * j + 7 + 2 * k, 8)
-        device = ring(-7 + 6 * k) if j == 0 else sib
-        return start(images.at[2 * j], images.at[slot], i_send.at[4 + j], i_recv.at[slot, 0], device)
-
-    i_copies.append(odd_image(0))
-
-    def i_edge(h):
-        return remote(images.at[8, halves[h]], images.at[2, halves[h]], i_send.at[8 + h], i_recv.at[2, h], ring(-8))
-
-    def i_inner(h, slot, n, delta):
-        rows = halves[h]
-        return remote(images.at[slot, rows], images.at[4, rows], i_send.at[n + h], i_recv.at[4, h], ring(delta))
-
-    def pass_on_images(h):
-        rows = halves[h]
-
-        @pl.when(y == 3)
-        def _():
-            landed(images.at[8, rows], i_recv.at[8, h])
-            i_edge(h).start()
-
-        landed(images.at[6, rows], i_recv.at[6, h])
-
-        @pl.when(y < 3)
-        def _():
-            landed(images.at[2, rows], i_recv.at[2, h])
-
-        @pl.when(inner)
-        def _():
-            i_inner(h, 6, 10, 2).start()
-            i_inner(h, 2, 12, -2).start()
-
-    pass_on_images(0)
+    @pl.when(jnp.logical_and(inner, z == 0))
+    def _():
+        image_copy(1).start()
+
+    i_copies = [odd_image(0)]
+
+    landed(images.at[6], i_recv.at[6])
+    landed(images.at[2], i_recv.at[2])
+
+    @pl.when(inner)
+    def _():
+        for copy in image_inner:
+            copy.start()
 
     part = lax.div(w, 4)
     own = total.at[block, part, 4 * y + lax.rem(w, 4)]
@@ -326,12 +334,19 @@
         for i in far_first:
             a_copy(i).start()
 
-    pass_on_images(1)
-    i_copies.append(odd_image(3))
-    landed(images.at[1], i_recv.at[1, 0])
+    i_copies += [odd_image(3), odd_image(1)]
+    landed(images.at[1], i_recv.at[1])
     gather_grad(texts[0], pair_of(images, 0, 1), True)
-    landed(images.at[7], i_recv.at[7, 0])
+    landed(images.at[7], i_recv.at[7])
     gather_grad(texts[0], pair_of(images, 6, 7), False)
+    landed(images.at[3 + 2 * k], i_recv.at[3 + 2 * k])
+    gather_grad(texts[0], pair_of(images, 2, 3 + 2 * k), False)
+
+    landed(images.at[4], i_recv.at[4])
+    i_copies.append(odd_image(2))
+    landed(images.at[5 - 2 * k], i_recv.at[5 - 2 * k])
+    gather_grad(texts[0], pair_of(images, 4, 5 - 2 * k), False)
+    gt_ref[...] = back_norm(text[...].astype(jnp.float32), t_sq, grad[...]).astype(jnp.bfloat16)
 
     first = part - lax.div(w, 12)
     last = lax.rem(lax.div(w, 6) + 2, 3)
@@ -348,21 +363,6 @@
         there = total.at[block, q, pl.ds(4 * y, 4)]
         for m, (i, j) in enumerate(plane):
             b_copies.append(start(there, there, b_send.at[n, m], b_recv.at[n, m], at(xs(i), z, ys(j), k)))
-
-    @pl.when(y == 3)
-    def _():
-        for h, rows in enumerate(halves):
-            landed(images.at[2, rows], i_recv.at[2, h])
-
-    i_copies.append(odd_image(1))
-    for h, rows in enumerate(halves):
-        landed(images.at[4, rows], i_recv.at[4, h])
-    i_copies.append(odd_image(2))
-    landed(images.at[3 + 2 * k], i_recv.at[3 + 2 * k, 0])
-    gather_grad(texts[0], pair_of(images, 2, 3 + 2 * k), False)
-    landed(images.at[5 - 2 * k], i_recv.at[5 - 2 * k, 0])
-    gather_grad(texts[0], pair_of(images, 4, 5 - 2 * k), False)
-    gt_ref[...] = back_norm(text[...].astype(jnp.float32), t_sq, grad[...]).astype(jnp.bfloat16)
 
     c_copies = []
     for n, q in enumerate(parts):
@@ -397,18 +397,20 @@
         for h in (0, 1):
             t_edge(h).wait_send()
 
+    image_copy(0).wait_send()
+    image_copy(1).wait_send()
+
     @pl.when(y == 3)
     def _():
-        for h in (0, 1):
-            i_edge(h).wait_send()
+        image_edge.wait_send()
 
     @pl.when(inner)
     def _():
         for h in (0, 1):
             t_inner(h, 6, 10, -2).wait_send()
             t_inner(h, 2, 12, 2).wait_send()
-            i_inner(h, 6, 10, 2).wait_send()
-            i_inner(h, 2, 12, -2).wait_send()
+        for copy in image_inner:
+            copy.wait_send()
 
     @pl.when(w < OWN)
     def _():
@@ -424,7 +426,7 @@
     sems = lambda *n: pltpu.SemaphoreType.DMA(n)
     grad_text, head = pl.pallas_call(
         kernel,
-        out_shape=(jax.ShapeDtypeStruct((B, D), bf16), jax.ShapeDtypeStruct((F, D), bf16)),
+        out_shape=(pltpu.VMEM((B, D), bf16), pltpu.VMEM((F, D), bf16)),
         in_specs=[any_spec] * 4 + [smem] * 2,
         out_specs=(vmem, vmem),
         scratch_shapes=[
@@ -446,7 +448,7 @@
             pltpu.VMEM((15, 16, 128), bf16),
             pltpu.VMEM((8, PARTS, 16, 16, 128), bf16),
             pltpu.VMEM((D, F), bf16),
-            pltpu.SemaphoreType.REGULAR((3,)), sems(4), sems(14), sems(9, 2), sems(14), sems(9, 2), sems(8), sems(8), sems(7), sems(7), sems(3), sems(3),
+            pltpu.SemaphoreType.REGULAR((3,)), sems(4), sems(14), sems(9, 2), sems(9), sems(9), sems(8), sems(8), sems(7), sems(7), sems(3), sems(3),
             sems(15), sems(15), sems(15), sems(12), sems(3, 15), sems(3, 15), sems(3, 4), sems(3, 4),
         ],
         compiler_params=pltpu.CompilerParams(

time: 83.2 us -> 76.6 us (0.921)
  Pallas kernels: 76.8 us -> 72.7 us
  local copies, waits for them, and re-layouts: 4.29 us -> 1.83 us
    pallas_call x1, Pallas kernels: 76.8 us -> 72.7 us  [on_device(): pl.pallas_call(kernel, out_shape=(pltpu.VMEM((B, D), bf16), pltpu.VMEM((F...]
    unnamed x2, local copies, waits for them, and re-layouts: 4.29 us -> 1.83 us
where the time goes in v3:
time: 76.6 us; the launch traced here: 76.4 us
  Pallas kernels  72.7 us (95%)
  between operations  1.93 us (3%)
  local copies, waits for them, and re-layouts  1.83 us (2%)
    pallas_call x1, Pallas kernels, on_device(): pl.pallas_call(kernel, out_shape=(pltpu.VMEM((B, D), bf16), pltpu.VMEM((F...  72.7 us
    unnamed x2, local copies, waits for them, and re-layouts  1.83 us

profile of v3, /device:TPU:1, one launch (start us, length us, event | category | flops | bytes accessed | tf_op | source)
XLA Modules:
  0.0 76.4 jit_solution(6152341652612034966)
XLA Ops:
  1.9 72.7 %shard_map.77 = (bf16[128,1152]{1,0:T(8,128)(2,1)S(1)}, bf16[640,1152]{1,0:T(8,128)(2,1)S(1)}) custom-call(bf16[128,640]{1,0:T(8,128)(2,1)} %feats_hbm.1, bf16[640,1152]{1,0:T(8,128)(2,1)} %proj_hbm.1, bf16[128,1152]{1,0:T(8,128)(2,1)} %rest_hbm.1, bf16[128,1152]{1,0:T(8,128)(2,1)} %text_hbm.1, f32[1]{0:T(128)S(6)} %copy.12.scale_ref, f32[1]{0:T(128)S(6)} %copy.13.bias_ref), custom_call_target="tpu_custom_call" | custom-call | tf_op jit(solution)/shard_map/pallas_call | solution.py:427
  74.6 0.7 copy.10
  75.3 1.1 %copy.11 = bf16[640,1152]{1,0:T(8,128)(2,1)} copy(bf16[640,1152]{1,0:T(8,128)(2,1)S(1)} %get-tuple-element.3) | data formatting | bytes 2949120

commit v4 on v3

--- a/solution.py
+++ b/solution.py
@@ -306,14 +306,6 @@
 
     i_copies = [odd_image(0)]
 
-    landed(images.at[6], i_recv.at[6])
-    landed(images.at[2], i_recv.at[2])
-
-    @pl.when(inner)
-    def _():
-        for copy in image_inner:
-            copy.start()
-
     part = lax.div(w, 4)
     own = total.at[block, part, 4 * y + lax.rem(w, 4)]
 
@@ -333,6 +325,14 @@
     def _():
         for i in far_first:
             a_copy(i).start()
+
+    landed(images.at[6], i_recv.at[6])
+    landed(images.at[2], i_recv.at[2])
+
+    @pl.when(inner)
+    def _():
+        for copy in image_inner:
+            copy.start()
 
     i_copies += [odd_image(3), odd_image(1)]
     landed(images.at[1], i_recv.at[1])
@@ -342,12 +342,6 @@
     landed(images.at[3 + 2 * k], i_recv.at[3 + 2 * k])
     gather_grad(texts[0], pair_of(images, 2, 3 + 2 * k), False)
 
-    landed(images.at[4], i_recv.at[4])
-    i_copies.append(odd_image(2))
-    landed(images.at[5 - 2 * k], i_recv.at[5 - 2 * k])
-    gather_grad(texts[0], pair_of(images, 4, 5 - 2 * k), False)
-    gt_ref[...] = back_norm(text[...].astype(jnp.float32), t_sq, grad[...]).astype(jnp.bfloat16)
-
     first = part - lax.div(w, 12)
     last = lax.rem(lax.div(w, 6) + 2, 3)
     b_copies = []
@@ -364,16 +358,22 @@
         for m, (i, j) in enumerate(plane):
             b_copies.append(start(there, there, b_send.at[n, m], b_recv.at[n, m], at(xs(i), z, ys(j), k)))
 
+    landed(images.at[4], i_recv.at[4])
+    i_copies.append(odd_image(2))
+    landed(images.at[5 - 2 * k], i_recv.at[5 - 2 * k])
+    gather_grad(texts[0], pair_of(images, 4, 5 - 2 * k), False)
+    gt_ref[...] = back_norm(text[...].astype(jnp.float32), t_sq, grad[...]).astype(jnp.bfloat16)
+
     c_copies = []
     for n, q in enumerate(parts):
-        for i in range(4):
+        for i in (0, 1, 3, 2):
             for m, (pi, pj) in enumerate(plane):
                 if pi == i:
                     landed(total.at[2 * xs(-pi) + k, q, pl.ds(4 * ys(-pj), 4)], b_recv.at[n, m])
             there = total.at[2 * xs(-i) + k, q]
             c_copies.append(start(there, there, c_send.at[n, i], c_recv.at[n, i], sib))
     for n, q in enumerate(parts):
-        for i in range(4):
+        for i in (0, 1, 3, 2):
             landed(total.at[2 * xs(-i) + 1 - k, q], c_recv.at[n, i])
     for b in range(8):
         for n in range(TILES):

time: 76.6 us -> 75.7 us (0.988)
  Pallas kernels: 72.7 us -> 71.8 us
    pallas_call x1, Pallas kernels: 72.7 us -> 71.8 us  [on_device(): pl.pallas_call(kernel, out_shape=(pltpu.VMEM((B, D), bf16), pltpu.VMEM((F...]
where the time goes in v4:
time: 75.7 us; the launch traced here: 75.5 us
  Pallas kernels  71.8 us (95%)
  between operations  1.93 us (3%)
  local copies, waits for them, and re-layouts  1.83 us (2%)
    pallas_call x1, Pallas kernels, on_device(): pl.pallas_call(kernel, out_shape=(pltpu.VMEM((B, D), bf16), pltpu.VMEM((F...  71.8 us
    unnamed x2, local copies, waits for them, and re-layouts  1.83 us

profile of v4, /device:TPU:1, one launch (start us, length us, event | category | flops | bytes accessed | tf_op | source)
XLA Modules:
  0.0 75.5 jit_solution(6321165893447675116)
XLA Ops:
  1.9 71.8 %shard_map.77 = (bf16[128,1152]{1,0:T(8,128)(2,1)S(1)}, bf16[640,1152]{1,0:T(8,128)(2,1)S(1)}) custom-call(bf16[128,640]{1,0:T(8,128)(2,1)} %feats_hbm.1, bf16[640,1152]{1,0:T(8,128)(2,1)} %proj_hbm.1, bf16[128,1152]{1,0:T(8,128)(2,1)} %rest_hbm.1, bf16[128,1152]{1,0:T(8,128)(2,1)} %text_hbm.1, f32[1]{0:T(128)S(6)} %copy.12.scale_ref, f32[1]{0:T(128)S(6)} %copy.13.bias_ref), custom_call_target="tpu_custom_call" | custom-call | tf_op jit(solution)/shard_map/pallas_call | solution.py:427
  73.7 0.7 copy.10
  74.4 1.1 %copy.11 = bf16[640,1152]{1,0:T(8,128)(2,1)} copy(bf16[640,1152]{1,0:T(8,128)(2,1)S(1)} %get-tuple-element.3) | data formatting | bytes 2949120

commit v5 on v4

--- a/solution.py
+++ b/solution.py
@@ -122,8 +122,8 @@
     t_copies = []
     for h, rows in enumerate(halves):
         slot = 2 + 6 * at_end
+        t_copies.append(start(texts.at[0, rows], texts.at[6, rows], t_send.at[2 + h], t_recv.at[6, h], ring(6)))
         t_copies.append(start(texts.at[0, rows], texts.at[slot, rows], t_send.at[h], t_recv.at[slot, h], ring(2 - 8 * at_end)))
-        t_copies.append(start(texts.at[0, rows], texts.at[6, rows], t_send.at[2 + h], t_recv.at[6, h], ring(6)))
 
     def odd_text(j):
         slot = lax.rem(2 * j + 9 - 2 * k, 8)
@@ -372,14 +372,19 @@
                     landed(total.at[2 * xs(-pi) + k, q, pl.ds(4 * ys(-pj), 4)], b_recv.at[n, m])
             there = total.at[2 * xs(-i) + k, q]
             c_copies.append(start(there, there, c_send.at[n, i], c_recv.at[n, i], sib))
+    def assemble(b):
+        base = pl.multiple_of(ROWS * b, 16)
+        for n in range(TILES):
+            i, j = n // 5, n % 5
+            headt[pl.ds(base + 16 * i, 16), 128 * j : 128 * j + 128] = total[b, n // 16, n % 16]
+
+    for i in (0, 1, 3, 2):
+        assemble(2 * xs(-i) + k)
     for n, q in enumerate(parts):
         for i in (0, 1, 3, 2):
             landed(total.at[2 * xs(-i) + 1 - k, q], c_recv.at[n, i])
-    for b in range(8):
-        for n in range(TILES):
-            i, j = n // 5, n % 5
-            headt[ROWS * b + 16 * i : ROWS * b + 16 * i + 16, 128 * j : 128 * j + 128] = total[b, n // 16, n % 16]
-
+    for i in (0, 1, 3, 2):
+        assemble(2 * xs(-i) + 1 - k)
     for i in range(9):
         for j in range(5):
             block_t = headt[128 * i : 128 * i + 128, 128 * j : 128 * j + 128].astype(jnp.float32)

time: 75.7 us -> 75.8 us (level)
  no operation moved by 1% of the time
where the time goes in v5:
time: 75.8 us; the launch traced here: 75.6 us
  Pallas kernels  71.9 us (95%)
  between operations  1.93 us (3%)
  local copies, waits for them, and re-layouts  1.83 us (2%)
    pallas_call x1, Pallas kernels, on_device(): pl.pallas_call(kernel, out_shape=(pltpu.VMEM((B, D), bf16), pltpu.VMEM((F...  71.9 us
    unnamed x2, local copies, waits for them, and re-layouts  1.83 us

profile of v5, /device:TPU:1, one launch (start us, length us, event | category | flops | bytes accessed | tf_op | source)
XLA Modules:
  0.0 75.6 jit_solution(9785464599722130351)
XLA Ops:
  1.9 71.9 %shard_map.77 = (bf16[128,1152]{1,0:T(8,128)(2,1)S(1)}, bf16[640,1152]{1,0:T(8,128)(2,1)S(1)}) custom-call(bf16[128,640]{1,0:T(8,128)(2,1)} %feats_hbm.1, bf16[640,1152]{1,0:T(8,128)(2,1)} %proj_hbm.1, bf16[128,1152]{1,0:T(8,128)(2,1)} %rest_hbm.1, bf16[128,1152]{1,0:T(8,128)(2,1)} %text_hbm.1, f32[1]{0:T(128)S(6)} %copy.12.scale_ref, f32[1]{0:T(128)S(6)} %copy.13.bias_ref), custom_call_target="tpu_custom_call" | custom-call | tf_op jit(solution)/shard_map/pallas_call | solution.py:432
  73.8 0.7 copy.10
  74.5 1.1 %copy.11 = bf16[640,1152]{1,0:T(8,128)(2,1)} copy(bf16[640,1152]{1,0:T(8,128)(2,1)S(1)} %get-tuple-element.3) | data formatting | bytes 2949120
